TPU v7x, 512 devices: a whole 4x8x8 slice. The times are simulated.
512 devices in a mesh: dp: 64 (over y, x, z_lo), tensor: 8 (over z_hi, core).
Axes of the slice: x: 4, y: 8, z: 8 (z_hi: 4, z_lo: 2; z = z_hi * 2 + z_lo), core: 2. Of those that a mesh axis runs over, the one named last changes fastest.
Arguments:
- activations: bfloat16 [128000, 512], P('dp'), may hold values from -26 to 26
- out_grad: bfloat16 [128000, 8192], P('dp', 'tensor'), may hold values from -0.07267221 to 0.07267221
- weight: float32 [512, 8192], P('dp', 'tensor'), may hold values from -0.25 to 0.25
- row_moment: float32 [512], P('dp'), may hold values from 0.08 to 1.24
- col_moment: float32 [8192], P('tensor'), may hold values from 0.1 to 1
Outputs:
- new_weight: float32 [512, 8192], P('dp', 'tensor')
- step_taken: float32 [512, 8192], P('dp', 'tensor')
- row_next: float32 [512], P('dp')
- col_next: float32 [8192], P('tensor')
- row_factor: float32 [512], P('dp')
All inputs are finite; a program needn't handle non-finite values.
Results may differ from a plain program's by a relative error of at most 0.0003.
Values sent between devices are 32-bit elements; how exact they have to be, the bound alone decides.
No kernel may reach another device: no remote copies, remote signals or barrier semaphores. Data moves between devices by JAX's collectives and lax.ppermute only.
A program may use at most 64 MiB of HBM per device.

v0:
```python
import jax
import jax.numpy as jnp
from jax import lax
from jax.sharding import PartitionSpec as P

tiny_square = 1e-30
decay_rate = 0.8
clip_level = 0.25
learn_rate = 0.01


def body(activations, out_grad, weight, row_moment, col_moment):
    own_rows = weight.shape[0]
    own_cols = weight.shape[1]
    all_rows = own_rows * lax.axis_size("dp")
    all_cols = own_cols * lax.axis_size("tensor")
    grad = lax.psum_scatter(
        lax.dot_general(
            activations, out_grad, (((0,), (0,)), ((), ())), preferred_element_type=jnp.float32
        ),
        "dp",
        scatter_dimension=0,
        tiled=True,
    )
    squares = grad * grad + tiny_square
    row_sq = lax.psum(jnp.sum(squares, axis=1), "tensor")
    col_sq = lax.psum(jnp.sum(squares, axis=0), "dp")
    row_next = decay_rate * row_moment + (1.0 - decay_rate) * row_sq / all_cols
    col_next = decay_rate * col_moment + (1.0 - decay_rate) * col_sq / all_rows
    row_mean = lax.psum(jnp.sum(row_next), "dp") / all_rows
    row_factor = row_next / row_mean
    scaled = grad / jnp.sqrt(row_next[:, None] * col_next[None, :] / row_mean)
    overall = lax.psum(jnp.sum(scaled * scaled), ("dp", "tensor"))
    rms = jnp.sqrt(overall / (all_rows * all_cols))
    step_taken = scaled / jnp.maximum(1.0, rms / clip_level)
    return (weight - learn_rate * step_taken, step_taken, row_next, col_next, row_factor)


def solution(mesh):
    return jax.shard_map(
        body,
        mesh=mesh,
        in_specs=(P("dp", None), P("dp", "tensor"), P("dp", "tensor"), P("dp"), P("tensor")),
        out_specs=(P("dp", "tensor"), P("dp", "tensor"), P("dp"), P("tensor"), P("dp")),
        check_vma=False,
    )
```

profile of v0, /device:TPU:1, one launch (start us, length us, event | category | flops | bytes accessed | tf_op | source)
XLA Modules:
  0.0 618.7 jit_solution(14049004026473683768)
XLA Ops:
  7.2 0.0 copy-start
  7.2 0.0 reduce-scatter.2.cloned.1.call-start
  7.2 1.5 copy-done
  8.7 5.9 fusion.3
  14.6 0.0 copy-start.5
  14.6 0.0 copy-start.4
  14.6 0.0 copy-start.2
  14.6 0.0 reduce-scatter.2.cloned.1.call-update
  14.6 276.2 %reduce-scatter.2.cloned.1.call-done = f32[8,1024]{1,0:T(8,128)} async-done(((f32[512,1024]{1,0:T(8,128)}), f32[8,1024]{1,0:T(8,128)}) %reduce-scatter.2.cloned.1.call-update) | async-done | bytes 32784 | tf_op jit(solution)/shard_map/reduce_scatter | solution.py:17
  290.9 0.9 fusion
  291.8 64.4 %psum.28 = f32[8]{0:T(128)S(1)} all-reduce(f32[8]{0:T(128)S(1)} %get-tuple-element.6), channel_id=1, replica_groups=mesh['dp'=64,'tensor'=8] {'tensor'}, use_global_device_ids=true, to_apply=%region_2.0 | all-reduce | flops 8 | bytes 64 | tf_op jit(solution)/shard_map/psum | solution.py:26
  356.1 0.0 copy-done.5
  356.1 0.6 fusion.2
  356.7 0.0 copy-start.3
  356.7 128.8 %all-reduce = (f32[]{:T(128)}, f32[1024]{0:T(1024)S(1)}) all-reduce(f32[]{:T(128)} %get-tuple-element.11, f32[1024]{0:T(1024)S(1)} %get-tuple-element.5), channel_id=1, replica_groups=mesh['dp'=64,'tensor'=8] {'dp'}, use_global_device_ids=true, to_apply=%region_6.0 | all-reduce | flops 1025 | bytes 8200 | tf_op jit(solution)/shard_map/psum | solution.py:30
  486.2 0.0 copy-done.4
  486.2 0.0 copy-start.1
  486.2 1.4 multiply_reduce_fusion
  487.7 0.5 broadcast_divide_fusion.1
  488.2 121.4 %psum.31 = f32[]{:T(128)} all-reduce(f32[]{:T(128)} %multiply_reduce_fusion), channel_id=1, replica_groups=mesh['dp'=64,'tensor'=8] {'dp','tensor'}, use_global_device_ids=true, to_apply=%region_8.0 | all-reduce | flops 1 | bytes 8 | tf_op jit(solution)/shard_map/psum | solution.py:33
  610.3 0.0 copy-done.2
  610.4 1.5 multiply_subtract_fusion
  611.8 0.0 copy-done.3
  611.8 0.0 copy-done.1
  (1 shorter events, 0.0 us)
Async XLA Ops:
  7.2 1.6 copy-start
  7.2 283.7 %reduce-scatter.2.cloned.1.call-start = ((), (), s32[]{:S(2)}) async-start(), calls=%async_computation.1 | async-start | bytes 2129920 | tf_op jit(solution)/shard_map/reduce_scatter | solution.py:17
  14.6 341.5 %copy-start.5 = (f32[8]{0:T(128)S(1)}, f32[8]{0:T(128)}, u32[]{:S(2)}) copy-start(f32[8]{0:T(128)} %param.8) | copy-start | bytes 100
  14.6 471.6 %copy-start.4 = (f32[1024]{0:T(1024)S(1)}, f32[1024]{0:T(1024)}, u32[]{:S(2)}) copy-start(f32[1024]{0:T(1024)} %param.9) | copy-start | bytes 12292
  14.6 595.7 %copy-start.2 = (f32[8,1024]{1,0:T(8,128)S(1)}, f32[8,1024]{1,0:T(8,128)}, u32[]{:S(2)}) copy-start(f32[8,1024]{1,0:T(8,128)} %param.7) | copy-start | bytes 98308
  356.7 255.1 %copy-start.3 = (f32[8]{0:T(128)}, f32[8]{0:T(128)S(1)}, u32[]{:S(2)}) copy-start(f32[8]{0:T(128)S(1)} %get-tuple-element.12) | copy-start | bytes 100
  486.2 125.6 %copy-start.1 = (f32[1024]{0:T(1024)}, f32[1024]{0:T(1024)S(1)}, u32[]{:S(2)}) copy-start(f32[1024]{0:T(1024)S(1)} %multiply_add_fusion.1) | copy-start | bytes 12292
Sparse Core Ops, SparseCore 0:
  14.8 276.0 reduce-scatter.1
where the time goes:
time: 620 us; the launch traced here: 619 us
  blocking collectives  315 us (51%)
  waiting for transfers between devices  276 us (45%)
  between operations  15.4 us (2%)
    reduce_scatter x1, waiting for transfers between devices, body(): lax.psum_scatter(lax.dot_general(activations, out_grad, (((0,), (0,)), ((...  276 us
    psum x1, blocking collectives, body(): row_mean = lax.psum(jnp.sum(row_next), 'dp') / all_rows  129 us
    psum x1, blocking collectives, body(): overall = lax.psum(jnp.sum(scaled * scaled), ('dp', 'tensor'))  121 us
    psum x1, blocking collectives, body(): row_sq = lax.psum(jnp.sum(squares, axis=1), 'tensor')  64.4 us
  transfers between devices with their start and end apart: 1, of which 1 were waited for; matrix products, arithmetic and copies ran while one was open for 0% of the time, Pallas kernels for 0%

commit v1 on v0

v1 whole, which is shorter than its diff:
```python
import jax
import jax.numpy as jnp
from jax import lax
from jax.sharding import PartitionSpec as P

tiny_square = 1e-30
decay_rate = 0.8
clip_level = 0.25
learn_rate = 0.01


def shared_sum(values, axis):
    members = lax.axis_size(axis)
    copies = jnp.broadcast_to(values[None], (members,) + values.shape)
    return jnp.sum(lax.all_to_all(copies, axis, 0, 0), axis=0)


def body(activations, out_grad, weight, row_moment, col_moment):
    own_rows = weight.shape[0]
    own_cols = weight.shape[1]
    owners = lax.axis_size("dp")
    all_rows = own_rows * owners
    all_cols = own_cols * lax.axis_size("tensor")
    partial = lax.dot_general(
        activations, out_grad, (((0,), (0,)), ((), ())), preferred_element_type=jnp.float32
    )
    pieces = lax.all_to_all(partial.reshape(owners, own_rows, own_cols), "dp", 0, 0)
    grad = jnp.sum(pieces, axis=0)
    squares = grad * grad + tiny_square
    col_sq = shared_sum(jnp.sum(squares, axis=0).reshape(-1, 128), "dp").reshape(own_cols)
    col_next = decay_rate * col_moment + (1.0 - decay_rate) * col_sq / all_rows
    row_sq = jnp.sum(squares, axis=1)
    row_scaled = jnp.sum(grad * grad / col_next[None, :], axis=1)
    rows = shared_sum(jnp.stack([row_sq, row_scaled]), "tensor")
    row_next = decay_rate * row_moment + (1.0 - decay_rate) * rows[0] / all_cols
    totals = shared_sum(jnp.stack([jnp.sum(row_next), jnp.sum(rows[1] / row_next)])[None], "dp")[0]
    row_mean = totals[0] / all_rows
    row_factor = row_next / row_mean
    rms = jnp.sqrt(totals[1] * row_mean / (all_rows * all_cols))
    scaled = grad / jnp.sqrt(row_next[:, None] * col_next[None, :] / row_mean)
    step_taken = scaled / jnp.maximum(1.0, rms / clip_level)
    return (weight - learn_rate * step_taken, step_taken, row_next, col_next, row_factor)


def solution(mesh):
    return jax.shard_map(
        body,
        mesh=mesh,
        in_specs=(P("dp", None), P("dp", "tensor"), P("dp", "tensor"), P("dp"), P("tensor")),
        out_specs=(P("dp", "tensor"), P("dp", "tensor"), P("dp"), P("tensor"), P("dp")),
        check_vma=False,
    )
```

time: 620 us -> 127 us (0.20)
  waiting for transfers between devices: 276 us -> 0 us
  blocking collectives: 315 us -> 113 us
  between operations: 15.4 us -> 2.04 us
    psum x3 -> x0, blocking collectives: 315 us -> none  [the longest x1 129 us: body(): row_mean = lax.psum(jnp.sum(row_next), 'dp') / all_rows]
    reduce_scatter x1 -> x0, waiting for transfers between devices: 276 us -> none  [body(): lax.psum_scatter(lax.dot_general(activations, out_grad, (((0,), (0,)), ((...]
    all_to_all x0 -> x4, blocking collectives: none -> 113 us  [the longest x1 61 us: body(): lax.all_to_all(partial.reshape(owners, own_rows, own_cols), 'dp', 0, 0)]
  transfers between devices with their start and end apart: 1 -> 0, of which waited for: 1 -> 0; matrix products, arithmetic and copies ran while one was open for 0% -> 0% of each run, Pallas kernels for 0% -> 0%
where the time goes in v1:
time: 127 us
  blocking collectives  113 us (89%)
  other arithmetic  5.32 us (4%)
  matrix products  4.5 us (4%)
  local copies, waits for them, and re-layouts  2.22 us (2%)
  between operations  2.04 us (2%)
    all_to_all x1, blocking collectives, body(): lax.all_to_all(partial.reshape(owners, own_rows, own_cols), 'dp', 0, 0)  61 us
    all_to_all x3, blocking collectives, shared_sum(): return jnp.sum(lax.all_to_all(copies, axis, 0, 0), axis=0)  51.6 us
    dot_general x1, matrix products, body(): lax.dot_general(activations, out_grad, (((0,), (0,)), ((), ())), preferre...  4.5 us

profile of v1, /device:TPU:1, one launch (start us, length us, event | category | flops | bytes accessed | tf_op | source)
XLA Modules:
  0.0 126.7 jit_solution(18242859320898089362)
XLA Ops:
  0.6 0.0 copy-start
  0.6 1.6 %copy-done = bf16[2000,512]{1,0:T(8,128)(2,1)S(1)} copy-done((bf16[2000,512]{1,0:T(8,128)(2,1)S(1)}, bf16[2000,512]{1,0:T(8,128)(2,1)}, u32[]{:S(2)}) %copy-start) | copy-done | bytes 2048024
  2.2 4.5 %convolution_bitcast_fusion = f32[64,8,1024]{2,1,0:T(8,128)S(1)} fusion(bf16[2000,512]{1,0:T(8,128)(2,1)S(1)} %copy-done, bf16[2000,1024]{1,0:T(8,128)(2,1)} %param.6), kind=kOutput, calls=%fused_computation | convolution fusion | flops 2097152000 | bytes 8241152 | tf_op jit(solution)/shard_map/dot_general | solution.py:24
  6.7 61.0 %all_to_all.20 = f32[64,8,1024]{2,1,0:T(8,128)} all-to-all(f32[64,8,1024]{2,1,0:T(8,128)S(1)} %convolution_bitcast_fusion), channel_id=1, replica_groups=mesh['dp'=64,'tensor'=8] {'dp'}, dimensions={0} | all-to-all | bytes 4194304 | tf_op jit(solution)/shard_map/all_to_all | solution.py:27
  67.7 0.0 copy-start.3
  67.7 0.0 copy-start.5
  67.7 0.0 copy-start.2
  67.7 1.8 %reduce_sum.83 = f32[8,1024]{1,0:T(8,128)S(1)} reduce(f32[64,8,1024]{2,1,0:T(8,128)} %all_to_all.20, f32[]{:T(128)} %constant.10.clone.1), dimensions={0}, to_apply=%region_0.0 | reduce | flops 516096 | bytes 2129924 | tf_op jit(solution)/shard_map/reduce_sum | solution.py:28
  69.5 18.3 %all_to_all.21 = f32[64,8,128]{2,1,0:T(8,128)S(1)} all-to-all(f32[64,8,128]{2,1,0:T(8,128)S(1)} %broadcast_in_dim.9), channel_id=1, replica_groups=mesh['dp'=64,'tensor'=8] {'dp'}, dimensions={0} | all-to-all | bytes 524288 | tf_op jit(solution)/shard_map/all_to_all | solution.py:15
  87.8 0.1 reduce_sum.86
  87.9 0.0 copy-done.3
  87.9 0.0 copy-start.1
  87.9 0.2 add_reduce_fusion.1
  88.1 20.0 %all_to_all.22 = f32[8,2,8]{2,1,0:T(2,128)S(1)} all-to-all(f32[8,2,8]{2,1,0:T(2,128)S(1)} %broadcast_in_dim.10), channel_id=1, replica_groups=mesh['dp'=64,'tensor'=8] {'tensor'}, dimensions={0} | all-to-all | bytes 1024 | tf_op jit(solution)/shard_map/all_to_all | solution.py:15
  108.1 0.0 copy-done.5
  108.1 0.6 fusion.1
  108.7 0.0 copy-start.4
  108.7 1.4 %pad_maximum_fusion.1 = f32[2]{0:T(128)S(1)} fusion(f32[1]{0:T(128)} %bitcast.8, f32[1]{0:T(128)} %bitcast.6), kind=kLoop, calls=%fused_computation.8 | loop fusion | flops 2 | bytes 16 | tf_op jit(solution)/shard_map/stack | solution.py:36
  110.1 13.4 %all_to_all.23 = f32[64,1,2]{2,1,0:T(1,128)S(1)} all-to-all(f32[64,1,2]{2,1,0:T(1,128)S(1)} %broadcast_in_dim.11), channel_id=1, replica_groups=mesh['dp'=64,'tensor'=8] {'dp'}, dimensions={0} | all-to-all | bytes 1024 | tf_op jit(solution)/shard_map/all_to_all | solution.py:15
  123.5 0.1 reduce_sum.91
  123.6 0.6 fusion.2
  125.5 0.5 broadcast_divide_fusion
  126.0 0.0 copy-done.2
  126.0 0.7 multiply_subtract_fusion
  126.7 0.0 copy-done.1
  126.7 0.0 copy-done.4
  (7 shorter events, 0.1 us)
Async XLA Ops:
  0.6 1.6 %copy-start = (bf16[2000,512]{1,0:T(8,128)(2,1)S(1)}, bf16[2000,512]{1,0:T(8,128)(2,1)}, u32[]{:S(2)}) copy-start(bf16[2000,512]{1,0:T(8,128)(2,1)} %param.5) | copy-start | bytes 6144004
  67.7 20.2 %copy-start.3 = (f32[1024]{0:T(1024)S(1)}, f32[1024]{0:T(1024)}, u32[]{:S(2)}) copy-start(f32[1024]{0:T(1024)} %param.9) | copy-start | bytes 12292
  67.7 40.4 %copy-start.5 = (f32[8]{0:T(128)S(1)}, f32[8]{0:T(128)}, u32[]{:S(2)}) copy-start(f32[8]{0:T(128)} %param.8) | copy-start | bytes 100
  67.7 58.3 %copy-start.2 = (f32[8,1024]{1,0:T(8,128)S(1)}, f32[8,1024]{1,0:T(8,128)}, u32[]{:S(2)}) copy-start(f32[8,1024]{1,0:T(8,128)} %param.7) | copy-start | bytes 98308
  87.9 38.8 %copy-start.1 = (f32[1024]{0:T(1024)}, f32[1024]{0:T(1024)S(1)}, u32[]{:S(2)}) copy-start(f32[1024]{0:T(1024)S(1)} %bitcast_add_fusion) | copy-start | bytes 12292
  108.7 18.0 %copy-start.4 = (f32[8]{0:T(128)}, f32[8]{0:T(128)S(1)}, u32[]{:S(2)}) copy-start(f32[8]{0:T(128)S(1)} %get-tuple-element.11) | copy-start | bytes 100

commit v2 on v0

v2 whole, which is shorter than its diff:
```python
import functools

import jax
import jax.numpy as jnp
from jax import lax
from jax.experimental import pallas as pl
from jax.experimental.pallas import tpu as pltpu
from jax.sharding import Mesh
from jax.sharding import PartitionSpec as P

tiny_square = 1e-30
decay_rate = 0.8
clip_level = 0.25
learn_rate = 0.01

FIRST = ("y_lo", "x", "z_lo")
SECOND = ("y_hi",)
DP = ("y_hi", "y_lo", "x", "z_lo")
TENSOR = ("z_hi", "core")
SIZES = (4, 2, 4, 2, 4, 2)
LANES = 128
MIB = 2**20

VMEM = pl.BlockSpec(memory_space=pltpu.VMEM)
SMEM = pl.BlockSpec(memory_space=pltpu.SMEM)


def product_kernel(outer, middle, act_ref, cot_ref, out_ref):
    value = lax.dot_general(
        act_ref[...], cot_ref[...], (((0,), (0,)), ((), ())), preferred_element_type=jnp.float32
    )
    run = out_ref.shape[1] // outer
    for o in range(outer):
        for m in range(middle):
            at = (o * middle + m) * run
            out_ref[m, o * run : (o + 1) * run, :] = value[at : at + run, :]


def product(activations, out_grad, outer, middle):
    tokens, rows = activations.shape
    cols = out_grad.shape[1]
    width = 256
    return pl.pallas_call(
        functools.partial(product_kernel, outer, middle),
        grid=(cols // width,),
        in_specs=[
            pl.BlockSpec((tokens, rows), lambda j: (0, 0)),
            pl.BlockSpec((tokens, width), lambda j: (0, j)),
        ],
        out_specs=pl.BlockSpec((middle, rows // middle, width), lambda j: (0, 0, j)),
        out_shape=jax.ShapeDtypeStruct((middle, rows // middle, cols), jnp.float32),
        compiler_params=pltpu.CompilerParams(vmem_limit_bytes=56 * MIB),
        name="product",
    )(activations, out_grad)


def split_kernel(pieces_ref, out_ref):
    owners, _, rows, width = out_ref.shape
    own = rows // owners
    for c in range(owners):
        at = slice(c * width, (c + 1) * width)
        block = jnp.sum(pieces_ref[:, :, at], axis=0)
        out_ref[c, 0] = block
        for owner in range(owners):
            out_ref[owner, 1, c * own : (c + 1) * own, :] = block[owner * own : (owner + 1) * own]


def column_kernel(pieces_ref, grad_ref, own_ref, copies_ref):
    grad = jnp.sum(pieces_ref[:, 0], axis=0)
    grad_ref[...] = grad
    own_ref[...] = jnp.sum(pieces_ref[:, 1], axis=0)
    sums = jnp.sum(grad * grad + tiny_square, axis=0, keepdims=True)
    copies_ref[...] = jnp.broadcast_to(sums[None], copies_ref.shape)


def row_kernel(all_rows, all_cols, each, place_ref, row_moment_ref, cols_ref, col_moment_ref, grad_ref, message_ref):
    place = place_ref[0]
    col_next = (
        decay_rate * col_moment_ref[place] + (1.0 - decay_rate) * jnp.sum(cols_ref[...], axis=0) / all_rows
    )
    grad = grad_ref[...]
    square = grad * grad
    both = jnp.concatenate([square + tiny_square, square / col_next], axis=0)
    width = both.shape[1]
    both = sum(both[:, at : at + LANES] for at in range(0, width, LANES))
    both = jnp.concatenate([both, jnp.zeros((LANES - both.shape[0], LANES), jnp.float32)], axis=0)
    sums = jnp.sum(both.T, axis=0, keepdims=True)
    lane = lax.broadcasted_iota(jnp.int32, sums.shape, 1)
    scale = decay_rate / (1.0 - decay_rate) * all_cols / each
    own = row_moment_ref.shape[0]
    for r in range(own):
        sums = sums + jnp.where(lane == place * own + r, scale * row_moment_ref[r], 0.0)
    parts = [sums] + [col_next[:, at : at + LANES] for at in range(0, width, LANES)]
    parts += [jnp.zeros((message_ref.shape[1] - len(parts), LANES), jnp.float32)]
    message_ref[...] = jnp.broadcast_to(jnp.concatenate(parts, axis=0)[None], message_ref.shape)


def to_lanes(column):
    n = column.shape[0]
    here = lax.broadcasted_iota(jnp.int32, (n, LANES), 0) == lax.broadcasted_iota(jnp.int32, (n, LANES), 1)
    return jnp.sum(jnp.where(here, jnp.broadcast_to(column, (n, LANES)), 0.0), axis=0)[:n]


def update_kernel(all_cols, place_ref, message_ref, own_ref, update_ref, row_ref, col_ref, rows_ref, copies_ref):
    place, mine = place_ref[0], place_ref[1]
    owners, _, width = col_ref.shape
    rows = own_ref.shape[0]
    own, each = rows // owners, message_ref.shape[0] // owners
    sums = jnp.sum(message_ref[:, 0], axis=0, keepdims=True)
    row_next = (1.0 - decay_rate) / all_cols * sums[:, :rows]
    total = jnp.sum(sums[:, rows : 2 * rows] / row_next, axis=1, keepdims=True)
    row_sum = jnp.sum(row_next, axis=1, keepdims=True)
    lane = lax.broadcasted_iota(jnp.int32, (1, LANES), 1)
    copies_ref[...] = jnp.broadcast_to(jnp.where(lane < LANES // 2, total, row_sum)[None], copies_ref.shape)
    wide = jnp.broadcast_to(row_next, (own, rows))
    lane = lax.broadcasted_iota(jnp.int32, (own, rows), 1)
    here = lax.broadcasted_iota(jnp.int32, (own, rows), 0) + place * own
    column = jnp.sum(jnp.where(lane == here, wide, 0.0), axis=1, keepdims=True)
    row_ref[...] = to_lanes(column)
    rows_ref[...] = jnp.broadcast_to(column, rows_ref.shape)
    for owner in range(owners):
        source = owner * each + mine
        parts = [message_ref[source, k + 1 : k + 2] for k in range(width // LANES)]
        col_next = jnp.concatenate(parts, axis=1)
        col_ref[owner] = col_next
        grad = own_ref[owner * own : (owner + 1) * own]
        update_ref[:, owner * width : (owner + 1) * width] = grad / jnp.sqrt(column * col_next)


def finish_kernel(all_rows, all_cols, sums_ref, update_ref, rows_ref, weight_ref, new_ref, step_ref, factor_ref):
    sums = jnp.sum(sums_ref[...], axis=0)
    total, row_mean = sums[:, 0:1], sums[:, LANES - 1 :] / all_rows
    rms = jnp.sqrt(total * row_mean / (all_rows * all_cols))
    step = update_ref[...] * (jnp.sqrt(row_mean) / jnp.maximum(1.0, rms / clip_level))
    step_ref[...] = step
    new_ref[...] = weight_ref[...] - learn_rate * step
    factor_ref[...] = to_lanes(rows_ref[:, 0:1] / row_mean)


def call(kernel, outs, ins, name):
    return pl.pallas_call(
        kernel,
        in_specs=ins,
        out_specs=[VMEM] * len(outs),
        out_shape=[jax.ShapeDtypeStruct(shape, jnp.float32) for shape in outs],
        compiler_params=pltpu.CompilerParams(vmem_limit_bytes=32 * MIB),
        name=name,
    )


def body(activations, out_grad, weight, row_moment, col_moment):
    own_rows, own_cols = weight.shape
    all_rows = own_rows * lax.axis_size(DP)
    all_cols = own_cols * lax.axis_size(TENSOR)
    first, second, tensor = lax.axis_size(FIRST), lax.axis_size(SECOND), lax.axis_size(TENSOR)
    rows, width = second * own_rows, own_cols // second
    place = jnp.stack([lax.axis_index(SECOND), lax.axis_index(TENSOR)]).astype(jnp.int32)

    partial = product(activations, out_grad, lax.axis_size(SECOND), first)
    pieces = lax.all_to_all(partial, FIRST, 0, 0)
    (pieces,) = call(split_kernel, [(second, 2, rows, width)], [VMEM], "split")(pieces)
    pieces = lax.all_to_all(pieces, SECOND, 0, 0)
    grad, own, copies = call(
        column_kernel, [(rows, width), (rows, width), (first, 1, width)], [VMEM], "columns"
    )(pieces)
    cols = lax.all_to_all(copies, FIRST, 0, 0)
    (message,) = call(
        functools.partial(row_kernel, all_rows, all_cols, tensor),
        [(second * tensor, 4, LANES)],
        [SMEM, SMEM, VMEM, VMEM, VMEM],
        "rows",
    )(place, row_moment, cols, col_moment.reshape(second, 1, width), grad)
    message = lax.all_to_all(message, SECOND + TENSOR, 0, 0)
    update, row_next, col_next, rows_wide, copies = call(
        functools.partial(update_kernel, all_cols),
        [(own_rows, own_cols), (own_rows,), (second, 1, width), (own_rows, LANES), (first, 1, LANES)],
        [SMEM, VMEM, VMEM],
        "update",
    )(place, message, own)
    sums = lax.all_to_all(copies, FIRST, 0, 0)
    new_weight, step_taken, row_factor = call(
        functools.partial(finish_kernel, all_rows, all_cols),
        [(own_rows, own_cols), (own_rows, own_cols), (own_rows,)],
        [VMEM] * 4,
        "finish",
    )(sums, update, rows_wide, weight)
    return new_weight, step_taken, row_next, col_next.reshape(own_cols), row_factor


def solution(mesh):
    physical = Mesh(mesh.devices.reshape(SIZES), DP + TENSOR)
    return jax.shard_map(
        body,
        mesh=physical,
        in_specs=(P(DP, None), P(DP, TENSOR), P(DP, TENSOR), P(DP), P(TENSOR)),
        out_specs=(P(DP, TENSOR), P(DP, TENSOR), P(DP), P(TENSOR), P(DP)),
        check_vma=False,
    )
```

time: 620 us -> 106 us (0.17)
  waiting for transfers between devices: 276 us -> 13.8 us
  blocking collectives: 315 us -> 68.2 us
  between operations: 15.4 us -> 0.66 us
  starting transfers between devices: 0.04 us -> 11.9 us
  Pallas kernels: 0 us -> 10.9 us
    psum x3 -> x0, blocking collectives: 315 us -> none  [the longest x1 129 us: body(): row_mean = lax.psum(jnp.sum(row_next), 'dp') / all_rows]
    reduce_scatter x1 -> x0, waiting for transfers between devices: 276 us -> none  [body(): lax.psum_scatter(lax.dot_general(activations, out_grad, (((0,), (0,)), ((...]
    all_to_all x0 -> x3, blocking collectives: none -> 68.2 us  [the longest x1 32.2 us: body(): pieces = lax.all_to_all(partial, FIRST, 0, 0)]
    all_to_all x0 -> x2, waiting for transfers between devices: none -> 13.8 us  [the longest x1 8.04 us: body(): pieces = lax.all_to_all(pieces, SECOND, 0, 0)]
    all_to_all x0 -> x2, starting transfers between devices: none -> 11.9 us  [the longest x1 7.27 us: body(): pieces = lax.all_to_all(pieces, SECOND, 0, 0)]
    pallas_call x0 -> x6, Pallas kernels: none -> 10.9 us  [the longest x1 6.6 us: product(): pl.pallas_call(functools.partial(product_kernel, outer, middle), grid=(co...]
  transfers between devices with their start and end apart: 1 -> 2, of which waited for: 1 -> 2; matrix products, arithmetic and copies ran while one was open for 0% -> 0% of each run, Pallas kernels for 0% -> 0%
where the time goes in v2:
time: 106 us
  blocking collectives  68.2 us (64%)
  waiting for transfers between devices  13.8 us (13%)
  starting transfers between devices  11.9 us (11%)
  Pallas kernels  10.9 us (10%)
    all_to_all x1, blocking collectives, body(): pieces = lax.all_to_all(partial, FIRST, 0, 0)  32.2 us
    all_to_all x1, blocking collectives, body(): message = lax.all_to_all(message, SECOND + TENSOR, 0, 0)  27.6 us
    all_to_all x1, blocking collectives, body(): sums = lax.all_to_all(copies, FIRST, 0, 0)  8.38 us
    all_to_all x1, waiting for transfers between devices, body(): pieces = lax.all_to_all(pieces, SECOND, 0, 0)  8.04 us
    all_to_all x1, starting transfers between devices, body(): pieces = lax.all_to_all(pieces, SECOND, 0, 0)  7.27 us
    pallas_call x1, Pallas kernels, product(): pl.pallas_call(functools.partial(product_kernel, outer, middle), grid=(co...  6.6 us
    all_to_all x1, waiting for transfers between devices, body(): cols = lax.all_to_all(copies, FIRST, 0, 0)  5.8 us
    all_to_all x1, starting transfers between devices, body(): cols = lax.all_to_all(copies, FIRST, 0, 0)  4.61 us
  transfers between devices with their start and end apart: 2, of which 2 were waited for; matrix products, arithmetic and copies ran while one was open for 0% of the time, Pallas kernels for 0%

profile of v2, /device:TPU:1, one launch (start us, length us, event | category | flops | bytes accessed | tf_op | source)
XLA Modules:
  0.0 105.5 jit_solution(8396700970606441874)
XLA Ops:
  0.6 6.6 %product.1 = f32[16,32,1024]{2,1,0:T(8,128)} custom-call(bf16[2000,512]{1,0:T(8,128)(2,1)} %act_ref.1, bf16[2000,1024]{1,0:T(8,128)(2,1)} %cot_ref.1), custom_call_target="tpu_custom_call" | custom-call | tf_op jit(solution)/shard_map/product/pallas_call | solution.py:43
  7.2 32.2 %all_to_all.25.pieces_ref = f32[16,32,1024]{2,1,0:T(8,128)S(1)} all-to-all(f32[16,32,1024]{2,1,0:T(8,128)} %product.1), channel_id=1, replica_groups=mesh['y_hi'=4,'y_lo'=2,'x'=4,'z_lo'=2,'z_hi'=4,'core'=2] {'y_lo','x','z_..., dimensions={0} | all-to-all | bytes 4194304 | tf_op jit(solution)/shard_map/all_to_all | solution.py:160
  39.4 0.0 copy-start.1
  39.4 0.0 copy-start.2
  39.4 0.0 copy-start
  39.4 0.8 split.1
  40.2 7.3 %all-to-all-start.1 = ((f32[4,2,32,256]{3,2,1,0:T(8,128)}), f32[4,2,32,256]{3,2,1,0:T(8,128)S(1)}, u32[]{:S(2)}, u32[]{:S(2)}) async-start(f32[4,2,32,256]{3,2,1,0:T(8,128)} %split.1), calls=%async_computation.1 | async-start | bytes 524288 | tf_op jit(solution)/shard_map/all_to_all | solution.py:162
  47.5 8.0 %all-to-all-done.1.pieces_ref = f32[4,2,32,256]{3,2,1,0:T(8,128)S(1)} async-done(((f32[4,2,32,256]{3,2,1,0:T(8,128)}), f32[4,2,32,256]{3,2,1,0:T(8,128)S(1)}, u32[]{:S(2)}, u32[]{:S(2)}) %all-to-all-start.1) | async-done | bytes 262176 | tf_op jit(solution)/shard_map/all_to_all | solution.py:162
  55.6 0.6 columns.1
  56.2 4.6 %all-to-all-start.2 = ((f32[16,1,256]{2,1,0:T(1,128)}), f32[16,1,256]{2,1,0:T(1,128)S(1)}, u32[]{:S(2)}, u32[]{:S(2)}) async-start(f32[16,1,256]{2,1,0:T(1,128)} %get-tuple-element.16), calls=%async_computation.2 | async-start | bytes 32768 | tf_op jit(solution)/shard_map/all_to_all | solution.py:166
  60.8 0.1 pad_add_fusion.place_ref
  60.9 5.8 %all-to-all-done.2.cols_ref = f32[16,1,256]{2,1,0:T(1,128)S(1)} async-done(((f32[16,1,256]{2,1,0:T(1,128)}), f32[16,1,256]{2,1,0:T(1,128)S(1)}, u32[]{:S(2)}, u32[]{:S(2)}) %all-to-all-start.2) | async-done | bytes 16416 | tf_op jit(solution)/shard_map/all_to_all | solution.py:166
  66.7 0.0 copy-done.1
  66.7 0.0 copy-done.2
  66.7 0.7 rows.1
  67.4 27.6 %all_to_all.26.message_ref = f32[32,4,128]{2,1,0:T(4,128)S(1)} all-to-all(f32[32,4,128]{2,1,0:T(4,128)S(1)} %rows.1), channel_id=1, replica_groups=mesh['y_hi'=4,'y_lo'=2,'x'=4,'z_lo'=2,'z_hi'=4,'core'=2] {'y_hi','z_hi',..., dimensions={0} | all-to-all | bytes 131072 | tf_op jit(solution)/shard_map/all_to_all | solution.py:173
  95.0 1.2 %update.1 = (f32[8,1024]{1,0:T(8,128)S(1)}, f32[8]{0:T(128)}, f32[4,1,256]{2,1,0:T(1,128)}, f32[8,128]{1,0:T(8,128)S(1)}, f32[16,1,128]{2,1,0:T(1,128)S(1)}) custom-call(s32[2]{0:T(128)S(1)} %pad_add_fusion.place_ref, f32[32,4,128]{2,1,0:T(4,128)S(1)} %all_to_all.26.message_ref, f32[32,256]{1,0:T(8,128)S(1)} %get-tuple-element.18.own_ref), custom_call_target="tpu_custom_call" | custom-call | tf_op jit(solution)/shard_map/update/pallas_call | solution.py:174
  96.2 8.4 %all_to_all.27.sums_ref = f32[16,1,128]{2,1,0:T(1,128)S(1)} all-to-all(f32[16,1,128]{2,1,0:T(1,128)S(1)} %get-tuple-element.19), channel_id=1, replica_groups=mesh['y_hi'=4,'y_lo'=2,'x'=4,'z_lo'=2,'z_hi'=4,'core'=2] {'y_lo','x','z_..., dimensions={0} | all-to-all | bytes 16384 | tf_op jit(solution)/shard_map/all_to_all | solution.py:180
  104.6 0.0 copy-done
  104.6 0.9 finish.1
Async XLA Ops:
  39.4 27.3 %copy-start.1 = (f32[1024]{0:T(1024)S(1)}, f32[1024]{0:T(1024)}, u32[]{:S(2)}) copy-start(f32[1024]{0:T(1024)} %param.9) | copy-start | bytes 12292
  39.4 27.3 %copy-start.2 = (f32[8]{0:T(128)S(1)}, f32[8]{0:T(128)}, u32[]{:S(2)}) copy-start(f32[8]{0:T(128)} %row_moment_ref.1) | copy-start | bytes 100
  39.4 65.2 %copy-start = (f32[8,1024]{1,0:T(8,128)S(1)}, f32[8,1024]{1,0:T(8,128)}, u32[]{:S(2)}) copy-start(f32[8,1024]{1,0:T(8,128)} %weight_ref.1) | copy-start | bytes 98308
  40.2 15.3 %all-to-all-start.1 = ((f32[4,2,32,256]{3,2,1,0:T(8,128)}), f32[4,2,32,256]{3,2,1,0:T(8,128)S(1)}, u32[]{:S(2)}, u32[]{:S(2)}) async-start(f32[4,2,32,256]{3,2,1,0:T(8,128)} %split.1), calls=%async_computation.1 | async-start | bytes 524288 | tf_op jit(solution)/shard_map/all_to_all | solution.py:162
  56.2 10.5 %all-to-all-start.2 = ((f32[16,1,256]{2,1,0:T(1,128)}), f32[16,1,256]{2,1,0:T(1,128)S(1)}, u32[]{:S(2)}, u32[]{:S(2)}) async-start(f32[16,1,256]{2,1,0:T(1,128)} %get-tuple-element.16), calls=%async_computation.2 | async-start | bytes 32768 | tf_op jit(solution)/shard_map/all_to_all | solution.py:166

commit v3 on v0

v3 whole, which is shorter than its diff:
```python
import functools

import jax
import jax.numpy as jnp
import numpy as np
from jax import lax
from jax.experimental import pallas as pl
from jax.experimental.pallas import tpu as pltpu
from jax.sharding import Mesh
from jax.sharding import PartitionSpec as P

tiny_square = 1e-30
decay_rate = 0.8
clip_level = 0.25
learn_rate = 0.01

FIRST = ("z_lo", "x", "y_lo")
SECOND = ("y_hi",)
DP = ("y_hi", "y_lo", "x", "z_lo")
TENSOR = ("z_hi", "core")
SIZES = (4, 2, 4, 2, 4, 2)
LANES = 128
MIB = 2**20

VMEM = pl.BlockSpec(memory_space=pltpu.VMEM)
SMEM = pl.BlockSpec(memory_space=pltpu.SMEM)


def product_kernel(chunk, act_hbm, cot_hbm, out_ref, act, cot, total, act_sems, cot_sems):
    tokens, cols = cot.shape
    members, block, _ = out_ref.shape
    owners, run = lax.axis_size(SECOND), block // lax.axis_size(SECOND)
    parts = [pl.ds(at, min(chunk, tokens - at)) for at in range(0, tokens, chunk)]
    copies = []
    for i, part in enumerate(parts):
        pair = (
            pltpu.make_async_copy(act_hbm.at[part], act.at[part], act_sems.at[i]),
            pltpu.make_async_copy(cot_hbm.at[part], cot.at[part], cot_sems.at[i]),
        )
        for copy in pair:
            copy.start()
        copies.append(pair)
    for i, part in enumerate(parts):
        for copy in copies[i]:
            copy.wait()
        value = jnp.dot(act[part].T, cot[part], preferred_element_type=jnp.float32)
        if i > 0:
            value = total[...] + value
        if i < len(parts) - 1:
            total[...] = value
    order = np.arange(members).reshape([lax.axis_size(name) for name in DP[1:]])
    order = order.transpose([DP[1:].index(name) for name in FIRST]).reshape(-1)
    for owner in range(owners):
        for member in range(members):
            at = (owner * members + int(order[member])) * run
            out_ref[member, owner * run : (owner + 1) * run, :] = value[at : at + run, :]


def product(activations, out_grad, members):
    tokens, rows = activations.shape
    cols = out_grad.shape[1]
    chunk = 512
    n = pl.cdiv(tokens, chunk)
    return pl.pallas_call(
        functools.partial(product_kernel, chunk),
        in_specs=[pl.BlockSpec(memory_space=pl.ANY)] * 2,
        out_specs=VMEM,
        out_shape=jax.ShapeDtypeStruct((members, rows // members, cols), jnp.float32),
        scratch_shapes=[
            pltpu.VMEM((tokens, rows), activations.dtype),
            pltpu.VMEM((tokens, cols), out_grad.dtype),
            pltpu.VMEM((rows, cols), jnp.float32),
            pltpu.SemaphoreType.DMA((n,)),
            pltpu.SemaphoreType.DMA((n,)),
        ],
        compiler_params=pltpu.CompilerParams(vmem_limit_bytes=56 * MIB),
        name="product",
    )(activations, out_grad)


def split_kernel(place_ref, row_moment_ref, pieces_ref, out_ref):
    place, own = place_ref[0], row_moment_ref.shape[0]
    cols = pieces_ref.shape[2]
    for at in range(0, cols, LANES):
        block = jnp.sum(pieces_ref[:, :, at : at + LANES], axis=0)
        out_ref[:, :, at : at + LANES] = jnp.broadcast_to(block[None], (out_ref.shape[0],) + block.shape)
    lane = lax.broadcasted_iota(jnp.int32, block.shape, 1)
    moments = jnp.zeros(block.shape, jnp.float32)
    for r in range(own):
        moments = jnp.where(lane == place * own + r, row_moment_ref[r], moments)
    out_ref[:, :, cols:] = jnp.broadcast_to(moments[None], (out_ref.shape[0],) + block.shape)


def column_kernel(pieces_ref, grad_ref, moment_ref, copies_ref):
    cols = grad_ref.shape[1]
    grad = jnp.sum(pieces_ref[:, :, :cols], axis=0)
    grad_ref[...] = grad
    moment_ref[...] = jnp.sum(pieces_ref[:, :1, cols:], axis=0)
    sums = jnp.sum(grad * grad + tiny_square, axis=0, keepdims=True)
    copies_ref[...] = jnp.broadcast_to(sums[None], copies_ref.shape)


def row_kernel(all_rows, all_cols, each, cols_ref, col_moment_ref, grad_ref, moment_ref, col_ref, message_ref):
    col_next = (
        decay_rate * col_moment_ref[...] + (1.0 - decay_rate) * jnp.sum(cols_ref[...], axis=0) / all_rows
    )
    col_ref[...] = col_next
    grad = grad_ref[...]
    rows, cols = grad.shape
    square = grad * grad
    both = jnp.concatenate([square + tiny_square, square / col_next], axis=0)
    both = sum(both[:, at : at + LANES] for at in range(0, cols, LANES))
    both = jnp.concatenate([both, jnp.zeros((LANES - 2 * rows, LANES), jnp.float32)], axis=0)
    sums = jnp.sum(both.T, axis=0, keepdims=True)
    sums = sums + (decay_rate / (1.0 - decay_rate) * all_cols / each) * moment_ref[...]
    message_ref[...] = jnp.broadcast_to(sums[None], message_ref.shape)


def to_lanes(column):
    n = column.shape[0]
    here = lax.broadcasted_iota(jnp.int32, (n, LANES), 0) == lax.broadcasted_iota(jnp.int32, (n, LANES), 1)
    return jnp.sum(jnp.where(here, jnp.broadcast_to(column, (n, LANES)), 0.0), axis=0)[:n]


def finish_kernel(
    all_rows, all_cols, place_ref, message_ref, col_ref, grad_ref, weight_ref, new_ref, step_ref, row_ref, factor_ref
):
    place, member = place_ref[0], place_ref[1]
    own, rows = weight_ref.shape[0], grad_ref.shape[0]
    blocks = all_rows // rows
    each = message_ref.shape[0] // blocks
    sums = jnp.sum(message_ref[:, 0].reshape(blocks, each, LANES), axis=1)
    row_next = (1.0 - decay_rate) / all_cols * sums[:, :rows]
    scaled = sums[:, rows : 2 * rows] / row_next
    total = jnp.sum(jnp.sum(scaled, axis=1, keepdims=True), axis=0, keepdims=True)
    row_mean = jnp.sum(jnp.sum(row_next, axis=1, keepdims=True), axis=0, keepdims=True) / all_rows
    mine = lax.broadcasted_iota(jnp.int32, row_next.shape, 0) == member
    row_next = jnp.sum(jnp.where(mine, row_next, 0.0), axis=0, keepdims=True)
    lane = lax.broadcasted_iota(jnp.int32, (own, rows), 1)
    here = lax.broadcasted_iota(jnp.int32, (own, rows), 0) + place * own
    column = jnp.sum(jnp.where(lane == here, jnp.broadcast_to(row_next, (own, rows)), 0.0), axis=1, keepdims=True)
    row_ref[...] = to_lanes(column)
    factor_ref[...] = to_lanes(column / row_mean)
    rms = jnp.sqrt(total * row_mean / (all_rows * all_cols))
    grad = grad_ref[pl.ds(pl.multiple_of(place * own, own), own), :]
    scaled = grad / jnp.sqrt(column * col_ref[...] / row_mean)
    step = scaled / jnp.maximum(1.0, rms / clip_level)
    step_ref[...] = step
    new_ref[...] = weight_ref[...] - learn_rate * step


def call(kernel, outs, ins, name):
    return pl.pallas_call(
        kernel,
        in_specs=ins,
        out_specs=[VMEM] * len(outs),
        out_shape=[jax.ShapeDtypeStruct(shape, jnp.float32) for shape in outs],
        compiler_params=pltpu.CompilerParams(vmem_limit_bytes=32 * MIB),
        name=name,
    )


def body(activations, out_grad, weight, row_moment, col_moment):
    own_rows, cols = weight.shape
    all_rows = own_rows * lax.axis_size(DP)
    all_cols = cols * lax.axis_size(TENSOR)
    first, second, tensor = lax.axis_size(FIRST), lax.axis_size(SECOND), lax.axis_size(TENSOR)
    rows = second * own_rows
    place = jnp.stack([lax.axis_index(SECOND), lax.axis_index(FIRST)]).astype(jnp.int32)

    pieces = lax.all_to_all(product(activations, out_grad, first), FIRST, 0, 0)
    (pieces,) = call(split_kernel, [(second, rows, cols + LANES)], [SMEM, SMEM, VMEM], "split")(
        place, row_moment, pieces
    )
    pieces = lax.all_to_all(pieces, SECOND, 0, 0)
    grad, moment, copies = call(
        column_kernel, [(rows, cols), (1, LANES), (first, 1, cols)], [VMEM], "columns"
    )(pieces)
    copies = lax.all_to_all(copies, FIRST, 0, 0)
    col_next, message = call(
        functools.partial(row_kernel, all_rows, all_cols, tensor),
        [(1, cols), (first * tensor, 1, LANES)],
        [VMEM] * 4,
        "rows",
    )(copies, col_moment.reshape(1, cols), grad, moment)
    message = lax.all_to_all(message, FIRST + TENSOR, 0, 0)
    new_weight, step_taken, row_next, row_factor = call(
        functools.partial(finish_kernel, all_rows, all_cols),
        [(own_rows, cols), (own_rows, cols), (own_rows,), (own_rows,)],
        [SMEM] + [VMEM] * 4,
        "finish",
    )(place, message, col_next, grad, weight)
    return new_weight, step_taken, row_next, col_next.reshape(cols), row_factor


def solution(mesh):
    physical = Mesh(mesh.devices.reshape(SIZES), DP + TENSOR)
    return jax.shard_map(
        body,
        mesh=physical,
        in_specs=(P(DP, None), P(DP, TENSOR), P(DP, TENSOR), P(DP), P(TENSOR)),
        out_specs=(P(DP, TENSOR), P(DP, TENSOR), P(DP), P(TENSOR), P(DP)),
        check_vma=False,
    )
```

time: 620 us -> 103 us (0.17)
  blocking collectives: 315 us -> 59.4 us
  waiting for transfers between devices: 276 us -> 25.8 us
  between operations: 15.4 us -> 0.68 us
  Pallas kernels: 0 us -> 8.27 us
  starting transfers between devices: 0.04 us -> 7.79 us
    psum x3 -> x0, blocking collectives: 315 us -> none  [the longest x1 129 us: body(): row_mean = lax.psum(jnp.sum(row_next), 'dp') / all_rows]
    reduce_scatter x1 -> x0, waiting for transfers between devices: 276 us -> none  [body(): lax.psum_scatter(lax.dot_general(activations, out_grad, (((0,), (0,)), ((...]
    all_to_all x0 -> x3, blocking collectives: none -> 59.4 us  [the longest x1 25.3 us: body(): message = lax.all_to_all(message, FIRST + TENSOR, 0, 0)]
    all_to_all x0 -> x1, waiting for transfers between devices: none -> 25.8 us  [body(): pieces = lax.all_to_all(product(activations, out_grad, first), FIRST, 0, 0)]
    pallas_call x0 -> x5, Pallas kernels: none -> 8.27 us  [the longest x1 5.4 us: product(): pl.pallas_call(functools.partial(product_kernel, chunk), in_specs=[pl.Blo...]
    all_to_all x0 -> x1, starting transfers between devices: none -> 7.79 us  [body(): pieces = lax.all_to_all(product(activations, out_grad, first), FIRST, 0, 0)]
where the time goes in v3:
time: 103 us
  blocking collectives  59.4 us (58%)
  waiting for transfers between devices  25.8 us (25%)
  Pallas kernels  8.27 us (8%)
  starting transfers between devices  7.79 us (8%)
    all_to_all x1, waiting for transfers between devices, body(): pieces = lax.all_to_all(product(activations, out_grad, first), FIRST, 0, 0)  25.8 us
    all_to_all x1, blocking collectives, body(): message = lax.all_to_all(message, FIRST + TENSOR, 0, 0)  25.3 us
    all_to_all x1, blocking collectives, body(): pieces = lax.all_to_all(pieces, SECOND, 0, 0)  21.8 us
    all_to_all x1, blocking collectives, body(): copies = lax.all_to_all(copies, FIRST, 0, 0)  12.3 us
    all_to_all x1, starting transfers between devices, body(): pieces = lax.all_to_all(product(activations, out_grad, first), FIRST, 0, 0)  7.79 us
    pallas_call x1, Pallas kernels, product(): pl.pallas_call(functools.partial(product_kernel, chunk), in_specs=[pl.Blo...  5.4 us
  transfers between devices with their start and end apart: 1, of which 1 were waited for; matrix products, arithmetic and copies ran while one was open for 0% of the time, Pallas kernels for 0%

profile of v3, /device:TPU:1, one launch (start us, length us, event | category | flops | bytes accessed | tf_op | source)
XLA Modules:
  0.0 102.6 jit_solution(1902767455010618524)
XLA Ops:
  0.6 5.4 %product.1 = f32[16,32,1024]{2,1,0:T(8,128)} custom-call(bf16[2000,512]{1,0:T(8,128)(2,1)} %act_hbm.1, bf16[2000,1024]{1,0:T(8,128)(2,1)} %cot_hbm.1), custom_call_target="tpu_custom_call" | custom-call | tf_op jit(solution)/shard_map/product/pallas_call | solution.py:64
  6.0 0.0 copy-start.3
  6.1 7.8 %all-to-all-start = ((f32[16,32,1024]{2,1,0:T(8,128)}), f32[16,32,1024]{2,1,0:T(8,128)S(1)}, u32[]{:S(2)}, u32[]{:S(2)}) async-start(f32[16,32,1024]{2,1,0:T(8,128)} %product.1), calls=%async_computation | async-start | bytes 4194304 | tf_op jit(solution)/shard_map/all_to_all | solution.py:171
  13.9 0.1 pad_add_fusion.place_ref
  13.9 0.0 copy-start.2
  13.9 0.0 copy-start
  13.9 25.8 %all-to-all-done.pieces_ref = f32[16,32,1024]{2,1,0:T(8,128)S(1)} async-done(((f32[16,32,1024]{2,1,0:T(8,128)}), f32[16,32,1024]{2,1,0:T(8,128)S(1)}, u32[]{:S(2)}, u32[]{:S(2)}) %all-to-all-start) | async-done | bytes 2097184 | tf_op jit(solution)/shard_map/all_to_all | solution.py:171
  39.7 0.0 copy-done.3
  39.7 0.7 split.1
  40.4 21.8 %all_to_all.20.pieces_ref = f32[4,32,1152]{2,1,0:T(8,128)S(1)} all-to-all(f32[4,32,1152]{2,1,0:T(8,128)S(1)} %split.1), channel_id=1, replica_groups=mesh['y_hi'=4,'y_lo'=2,'x'=4,'z_lo'=2,'z_hi'=4,'core'=2] {'y_hi'}, dimensions={0} | all-to-all | bytes 1179648 | tf_op jit(solution)/shard_map/all_to_all | solution.py:175
  62.2 12.3 %all_to_all.21.cols_ref = f32[16,1,1024]{2,1,0:T(1,128)S(1)} all-to-all(f32[16,1,1024]{2,1,0:T(1,128)S(1)} %get-tuple-element.14), channel_id=1, replica_groups=mesh['y_hi'=4,'y_lo'=2,'x'=4,'z_lo'=2,'z_hi'=4,'core'=2] {'z_lo','x','y_..., dimensions={0} | all-to-all | bytes 131072 | tf_op jit(solution)/shard_map/all_to_all | solution.py:179
  74.5 0.0 copy-done.2
  74.5 0.7 rows.1
  75.2 25.3 %all_to_all.22.message_ref = f32[128,1,128]{2,1,0:T(1,128)S(1)} all-to-all(f32[128,1,128]{2,1,0:T(1,128)S(1)} %get-tuple-element.17), channel_id=1, replica_groups=mesh['y_hi'=4,'y_lo'=2,'x'=4,'z_lo'=2,'z_hi'=4,'core'=2] {'z_lo','x','y_..., dimensions={0} | all-to-all | bytes 131072 | tf_op jit(solution)/shard_map/all_to_all | solution.py:186
  100.5 0.0 copy-done
  100.5 0.0 copy-start.1
  100.5 0.7 copy-done.1
  101.2 1.5 %finish.1 = (f32[8,1024]{1,0:T(8,128)}, f32[8,1024]{1,0:T(8,128)}, f32[8]{0:T(128)}, f32[8]{0:T(128)}) custom-call(s32[2]{0:T(128)S(1)} %pad_add_fusion.place_ref, f32[128,1,128]{2,1,0:T(1,128)S(1)} %all_to_all.22.message_ref, f32[1,1024]{1,0:T(1,128)S(1)} %copy-done.1, f32[32,1024]{1,0:T(8,128)S(1)} %get-tuple-element.15.grad_ref, f32[8,1024]{1,0:T(8,128)S(1)} %copy-done), custom_call_target="tpu_custom_call" | custom-call | tf_op jit(solution)/shard_map/finish/pallas_call | solution.py:187
  (1 shorter events, 0.0 us)
Async XLA Ops:
  6.0 33.7 %copy-start.3 = (f32[8]{0:T(128)S(1)}, f32[8]{0:T(128)}, u32[]{:S(2)}) copy-start(f32[8]{0:T(128)} %row_moment_ref.1) | copy-start | bytes 100
  6.1 33.7 %all-to-all-start = ((f32[16,32,1024]{2,1,0:T(8,128)}), f32[16,32,1024]{2,1,0:T(8,128)S(1)}, u32[]{:S(2)}, u32[]{:S(2)}) async-start(f32[16,32,1024]{2,1,0:T(8,128)} %product.1), calls=%async_computation | async-start | bytes 4194304 | tf_op jit(solution)/shard_map/all_to_all | solution.py:171
  13.9 60.6 %copy-start.2 = (f32[1024]{0:T(1024)S(1)}, f32[1024]{0:T(1024)}, u32[]{:S(2)}) copy-start(f32[1024]{0:T(1024)} %param.9) | copy-start | bytes 12292
  13.9 86.5 %copy-start = (f32[8,1024]{1,0:T(8,128)S(1)}, f32[8,1024]{1,0:T(8,128)}, u32[]{:S(2)}) copy-start(f32[8,1024]{1,0:T(8,128)} %weight_ref.1) | copy-start | bytes 98308
  100.5 0.7 copy-start.1

commit v4 on v3

--- a/solution.py
+++ b/solution.py
@@ -14,7 +14,7 @@
 clip_level = 0.25
 learn_rate = 0.01
 
-FIRST = ("z_lo", "x", "y_lo")
+FIRST = ("z_lo", "y_lo", "x")
 SECOND = ("y_hi",)
 DP = ("y_hi", "y_lo", "x", "z_lo")
 TENSOR = ("z_hi", "core")
@@ -78,26 +78,28 @@
     )(activations, out_grad)
 
 
-def split_kernel(place_ref, row_moment_ref, pieces_ref, out_ref):
-    place, own = place_ref[0], row_moment_ref.shape[0]
-    cols = pieces_ref.shape[2]
-    for at in range(0, cols, LANES):
-        block = jnp.sum(pieces_ref[:, :, at : at + LANES], axis=0)
-        out_ref[:, :, at : at + LANES] = jnp.broadcast_to(block[None], (out_ref.shape[0],) + block.shape)
-    lane = lax.broadcasted_iota(jnp.int32, block.shape, 1)
-    moments = jnp.zeros(block.shape, jnp.float32)
+def split_kernel(row_moment_ref, pieces_ref, out_ref):
+    own, rows, cols = row_moment_ref.shape[1], pieces_ref.shape[1], pieces_ref.shape[2]
+    members, place = out_ref.shape[0], lax.axis_index(SECOND)
+    for c in range(cols // LANES):
+        block = jnp.sum(pieces_ref[:, :, c * LANES : (c + 1) * LANES], axis=0)
+        out_ref[:, c * rows : (c + 1) * rows, :] = jnp.broadcast_to(block[None], (members,) + block.shape)
+    lane = lax.broadcasted_iota(jnp.int32, (8, LANES), 1)
+    moments = jnp.zeros((8, LANES), jnp.float32)
     for r in range(own):
-        moments = jnp.where(lane == place * own + r, row_moment_ref[r], moments)
-    out_ref[:, :, cols:] = jnp.broadcast_to(moments[None], (out_ref.shape[0],) + block.shape)
+        moments = jnp.where(lane == place * own + r, row_moment_ref[:, r : r + 1], moments)
+    out_ref[:, cols // LANES * rows :, :] = jnp.broadcast_to(moments[None], (members, 8, LANES))
 
 
 def column_kernel(pieces_ref, grad_ref, moment_ref, copies_ref):
-    cols = grad_ref.shape[1]
-    grad = jnp.sum(pieces_ref[:, :, :cols], axis=0)
-    grad_ref[...] = grad
-    moment_ref[...] = jnp.sum(pieces_ref[:, :1, cols:], axis=0)
-    sums = jnp.sum(grad * grad + tiny_square, axis=0, keepdims=True)
-    copies_ref[...] = jnp.broadcast_to(sums[None], copies_ref.shape)
+    rows, cols = grad_ref.shape
+    for c in range(cols // LANES):
+        at = slice(c * LANES, (c + 1) * LANES)
+        grad = jnp.sum(pieces_ref[:, c * rows : (c + 1) * rows], axis=0)
+        grad_ref[:, at] = grad
+        sums = jnp.sum(grad * grad + tiny_square, axis=0, keepdims=True)
+        copies_ref[:, :, at] = jnp.broadcast_to(sums[None], (copies_ref.shape[0], 1, LANES))
+    moment_ref[...] = jnp.sum(pieces_ref[:, cols // LANES * rows :], axis=0)[:1]
 
 
 def row_kernel(all_rows, all_cols, each, cols_ref, col_moment_ref, grad_ref, moment_ref, col_ref, message_ref):
@@ -123,9 +125,9 @@
 
 
 def finish_kernel(
-    all_rows, all_cols, place_ref, message_ref, col_ref, grad_ref, weight_ref, new_ref, step_ref, row_ref, factor_ref
+    all_rows, all_cols, message_ref, kept_ref, grad_ref, weight_ref, new_ref, step_ref, row_ref, col_ref, factor_ref
 ):
-    place, member = place_ref[0], place_ref[1]
+    place, member = lax.axis_index(SECOND), lax.axis_index(FIRST)
     own, rows = weight_ref.shape[0], grad_ref.shape[0]
     blocks = all_rows // rows
     each = message_ref.shape[0] // blocks
@@ -143,7 +145,9 @@
     factor_ref[...] = to_lanes(column / row_mean)
     rms = jnp.sqrt(total * row_mean / (all_rows * all_cols))
     grad = grad_ref[pl.ds(pl.multiple_of(place * own, own), own), :]
-    scaled = grad / jnp.sqrt(column * col_ref[...] / row_mean)
+    col_next = kept_ref[...]
+    col_ref[...] = col_next
+    scaled = grad / jnp.sqrt(column * col_next / row_mean)
     step = scaled / jnp.maximum(1.0, rms / clip_level)
     step_ref[...] = step
     new_ref[...] = weight_ref[...] - learn_rate * step
@@ -166,30 +170,29 @@
     all_cols = cols * lax.axis_size(TENSOR)
     first, second, tensor = lax.axis_size(FIRST), lax.axis_size(SECOND), lax.axis_size(TENSOR)
     rows = second * own_rows
-    place = jnp.stack([lax.axis_index(SECOND), lax.axis_index(FIRST)]).astype(jnp.int32)
 
     pieces = lax.all_to_all(product(activations, out_grad, first), FIRST, 0, 0)
-    (pieces,) = call(split_kernel, [(second, rows, cols + LANES)], [SMEM, SMEM, VMEM], "split")(
-        place, row_moment, pieces
+    (pieces,) = call(split_kernel, [(second, rows * cols // LANES + 8, LANES)], [VMEM] * 2, "split")(
+        row_moment.reshape(1, own_rows), pieces
     )
     pieces = lax.all_to_all(pieces, SECOND, 0, 0)
     grad, moment, copies = call(
         column_kernel, [(rows, cols), (1, LANES), (first, 1, cols)], [VMEM], "columns"
     )(pieces)
     copies = lax.all_to_all(copies, FIRST, 0, 0)
-    col_next, message = call(
+    kept, message = call(
         functools.partial(row_kernel, all_rows, all_cols, tensor),
         [(1, cols), (first * tensor, 1, LANES)],
         [VMEM] * 4,
         "rows",
     )(copies, col_moment.reshape(1, cols), grad, moment)
     message = lax.all_to_all(message, FIRST + TENSOR, 0, 0)
-    new_weight, step_taken, row_next, row_factor = call(
+    new_weight, step_taken, row_next, col_next, row_factor = call(
         functools.partial(finish_kernel, all_rows, all_cols),
-        [(own_rows, cols), (own_rows, cols), (own_rows,), (own_rows,)],
-        [SMEM] + [VMEM] * 4,
+        [(own_rows, cols), (own_rows, cols), (own_rows,), (1, cols), (own_rows,)],
+        [VMEM] * 4,
         "finish",
-    )(place, message, col_next, grad, weight)
+    )(message, kept, grad, weight)
     return new_weight, step_taken, row_next, col_next.reshape(cols), row_factor
 
 

time: 103 us -> 97.4 us (0.946)
  blocking collectives: 59.4 us -> 89.6 us
  waiting for transfers between devices: 25.8 us -> 0 us
  starting transfers between devices: 7.79 us -> 0 us
  Pallas kernels: 8.27 us -> 6.74 us
    all_to_all x0 -> x1, blocking collectives: none -> 33.1 us  [body(): pieces = lax.all_to_all(product(activations, out_grad, first), FIRST, 0, 0)]
    all_to_all x1 -> x0, waiting for transfers between devices: 25.8 us -> none  [body(): pieces = lax.all_to_all(product(activations, out_grad, first), FIRST, 0, 0)]
    all_to_all x1 -> x0, starting transfers between devices: 7.79 us -> none  [body(): pieces = lax.all_to_all(product(activations, out_grad, first), FIRST, 0, 0)]
    all_to_all x1, blocking collectives: 12.3 us -> 8.88 us  [body(): copies = lax.all_to_all(copies, FIRST, 0, 0)]
    all_to_all x1, blocking collectives: 21.8 us -> 22.9 us  [body(): pieces = lax.all_to_all(pieces, SECOND, 0, 0)]
  transfers between devices with their start and end apart: 1 -> 0, of which waited for: 1 -> 0; matrix products, arithmetic and copies ran while one was open for 0% -> 0% of each run, Pallas kernels for 0% -> 0%
where the time goes in v4:
time: 97.4 us; the launch traced here: 97.1 us
  blocking collectives  89.6 us (92%)
  Pallas kernels  6.74 us (7%)
    all_to_all x1, blocking collectives, body(): pieces = lax.all_to_all(product(activations, out_grad, first), FIRST, 0, 0)  33.1 us
    all_to_all x1, blocking collectives, body(): message = lax.all_to_all(message, FIRST + TENSOR, 0, 0)  24.8 us
    all_to_all x1, blocking collectives, body(): pieces = lax.all_to_all(pieces, SECOND, 0, 0)  22.9 us
    all_to_all x1, blocking collectives, body(): copies = lax.all_to_all(copies, FIRST, 0, 0)  8.88 us
    pallas_call x1, Pallas kernels, product(): pl.pallas_call(functools.partial(product_kernel, chunk), in_specs=[pl.Blo...  5.4 us

profile of v4, /device:TPU:1, one launch (start us, length us, event | category | flops | bytes accessed | tf_op | source)
XLA Modules:
  0.0 97.1 jit_solution(2923299475145809552)
XLA Ops:
  0.6 5.4 %product.1 = f32[16,32,1024]{2,1,0:T(8,128)} custom-call(bf16[2000,512]{1,0:T(8,128)(2,1)} %act_hbm.1, bf16[2000,1024]{1,0:T(8,128)(2,1)} %cot_hbm.1), custom_call_target="tpu_custom_call" | custom-call | tf_op jit(solution)/shard_map/product/pallas_call | solution.py:64
  6.0 0.0 copy-start.2
  6.1 33.1 %all_to_all.20.pieces_ref = f32[16,32,1024]{2,1,0:T(8,128)S(1)} all-to-all(f32[16,32,1024]{2,1,0:T(8,128)} %product.1), channel_id=1, replica_groups=mesh['y_hi'=4,'y_lo'=2,'x'=4,'z_lo'=2,'z_hi'=4,'core'=2] {'z_lo','y_lo',..., dimensions={0} | all-to-all | bytes 4194304 | tf_op jit(solution)/shard_map/all_to_all | solution.py:174
  39.1 0.0 copy-done.2
  39.1 0.0 copy-start.1
  39.1 0.0 copy-start
  39.1 0.1 split.1
  39.3 22.9 %all_to_all.21.pieces_ref = f32[4,264,128]{2,1,0:T(8,128)S(1)} all-to-all(f32[4,264,128]{2,1,0:T(8,128)S(1)} %split.1), channel_id=1, replica_groups=mesh['y_hi'=4,'y_lo'=2,'x'=4,'z_lo'=2,'z_hi'=4,'core'=2] {'y_hi'}, dimensions={0} | all-to-all | bytes 1081344 | tf_op jit(solution)/shard_map/all_to_all | solution.py:178
  62.2 0.1 columns.1
  62.2 8.9 %all_to_all.22.cols_ref = f32[16,1,1024]{2,1,0:T(1,128)S(1)} all-to-all(f32[16,1,1024]{2,1,0:T(1,128)S(1)} %get-tuple-element.15), channel_id=1, replica_groups=mesh['y_hi'=4,'y_lo'=2,'x'=4,'z_lo'=2,'z_hi'=4,'core'=2] {'z_lo','y_lo',..., dimensions={0} | all-to-all | bytes 131072 | tf_op jit(solution)/shard_map/all_to_all | solution.py:182
  71.1 0.0 copy-done.1
  71.1 0.2 rows.1
  71.3 24.8 %all_to_all.23.message_ref = f32[128,1,128]{2,1,0:T(1,128)S(1)} all-to-all(f32[128,1,128]{2,1,0:T(1,128)S(1)} %get-tuple-element.18), channel_id=1, replica_groups=mesh['y_hi'=4,'y_lo'=2,'x'=4,'z_lo'=2,'z_hi'=4,'core'=2] {'z_lo','y_lo',..., dimensions={0} | all-to-all | bytes 131072 | tf_op jit(solution)/shard_map/all_to_all | solution.py:189
  96.1 0.0 copy-done
  96.1 0.9 finish.1
Async XLA Ops:
  6.0 33.1 %copy-start.2 = (f32[8]{0:T(128)S(1)}, f32[8]{0:T(128)}, u32[]{:S(2)}) copy-start(f32[8]{0:T(128)} %param.8) | copy-start | bytes 100
  39.1 32.0 %copy-start.1 = (f32[1024]{0:T(1024)S(1)}, f32[1024]{0:T(1024)}, u32[]{:S(2)}) copy-start(f32[1024]{0:T(1024)} %param.9) | copy-start | bytes 12292
  39.1 57.0 %copy-start = (f32[8,1024]{1,0:T(8,128)S(1)}, f32[8,1024]{1,0:T(8,128)}, u32[]{:S(2)}) copy-start(f32[8,1024]{1,0:T(8,128)} %weight_ref.1) | copy-start | bytes 98308

commit v5 on v4

--- a/solution.py
+++ b/solution.py
@@ -1,4 +1,5 @@
 import functools
+import math
 
 import jax
 import jax.numpy as jnp
@@ -26,10 +27,12 @@
 SMEM = pl.BlockSpec(memory_space=pltpu.SMEM)
 
 
-def product_kernel(chunk, act_hbm, cot_hbm, out_ref, act, cot, total, act_sems, cot_sems):
+def product_kernel(chunk, width, act_hbm, cot_hbm, out_hbm, act, cot, total, out, act_sems, cot_sems, out_sems):
     tokens, cols = cot.shape
-    members, block, _ = out_ref.shape
+    members, block, _ = out.shape
     owners, run = lax.axis_size(SECOND), block // lax.axis_size(SECOND)
+    order = np.arange(members).reshape([lax.axis_size(name) for name in DP[1:]])
+    order = order.transpose([DP[1:].index(name) for name in FIRST]).reshape(-1)
     parts = [pl.ds(at, min(chunk, tokens - at)) for at in range(0, tokens, chunk)]
     copies = []
     for i, part in enumerate(parts):
@@ -40,38 +43,49 @@
         for copy in pair:
             copy.start()
         copies.append(pair)
-    for i, part in enumerate(parts):
+    for i, part in enumerate(parts[:-1]):
         for copy in copies[i]:
             copy.wait()
         value = jnp.dot(act[part].T, cot[part], preferred_element_type=jnp.float32)
-        if i > 0:
-            value = total[...] + value
-        if i < len(parts) - 1:
-            total[...] = value
-    order = np.arange(members).reshape([lax.axis_size(name) for name in DP[1:]])
-    order = order.transpose([DP[1:].index(name) for name in FIRST]).reshape(-1)
-    for owner in range(owners):
-        for member in range(members):
-            at = (owner * members + int(order[member])) * run
-            out_ref[member, owner * run : (owner + 1) * run, :] = value[at : at + run, :]
+        total[...] = value if i == 0 else total[...] + value
+    for copy in copies[-1]:
+        copy.wait()
+    left = act[parts[-1]].T
+    results = []
+    for j, at in enumerate(range(0, cols, width)):
+        here = slice(at, at + width)
+        value = total[:, here] + jnp.dot(left, cot[parts[-1], here], preferred_element_type=jnp.float32)
+        for owner in range(owners):
+            for member in range(members):
+                row = (owner * members + int(order[member])) * run
+                out[member, owner * run : (owner + 1) * run, here] = value[row : row + run, :]
+        columns = pl.ds(at, width)
+        copy = pltpu.make_async_copy(out.at[:, :, columns], out_hbm.at[:, :, columns], out_sems.at[j])
+        copy.start()
+        results.append(copy)
+    for copy in results:
+        copy.wait()
 
 
 def product(activations, out_grad, members):
     tokens, rows = activations.shape
     cols = out_grad.shape[1]
-    chunk = 512
+    chunk, width = 512, 256
     n = pl.cdiv(tokens, chunk)
+    shape = (members, rows // members, cols)
     return pl.pallas_call(
-        functools.partial(product_kernel, chunk),
+        functools.partial(product_kernel, chunk, width),
         in_specs=[pl.BlockSpec(memory_space=pl.ANY)] * 2,
-        out_specs=VMEM,
-        out_shape=jax.ShapeDtypeStruct((members, rows // members, cols), jnp.float32),
+        out_specs=pl.BlockSpec(memory_space=pl.ANY),
+        out_shape=jax.ShapeDtypeStruct(shape, jnp.float32),
         scratch_shapes=[
             pltpu.VMEM((tokens, rows), activations.dtype),
             pltpu.VMEM((tokens, cols), out_grad.dtype),
             pltpu.VMEM((rows, cols), jnp.float32),
+            pltpu.VMEM(shape, jnp.float32),
             pltpu.SemaphoreType.DMA((n,)),
             pltpu.SemaphoreType.DMA((n,)),
+            pltpu.SemaphoreType.DMA((cols // width,)),
         ],
         compiler_params=pltpu.CompilerParams(vmem_limit_bytes=56 * MIB),
         name="product",
@@ -175,7 +189,9 @@
     (pieces,) = call(split_kernel, [(second, rows * cols // LANES + 8, LANES)], [VMEM] * 2, "split")(
         row_moment.reshape(1, own_rows), pieces
     )
-    pieces = lax.all_to_all(pieces, SECOND, 0, 0)
+    places = np.arange(math.prod(SIZES)).reshape(second, -1, SIZES[-1])
+    groups = [[int(d) for d in places[:: 1 - 2 * core, i, core]] for i in range(places.shape[1]) for core in range(SIZES[-1])]
+    pieces = lax.all_to_all(pieces, DP + TENSOR, 0, 0, axis_index_groups=groups)
     grad, moment, copies = call(
         column_kernel, [(rows, cols), (1, LANES), (first, 1, cols)], [VMEM], "columns"
     )(pieces)

time: 97.4 us -> 95.4 us (0.979)
  blocking collectives: 89.6 us -> 87.9 us
    all_to_all x1, blocking collectives: 22.9 us -> 20.7 us  [body(): pieces = lax.all_to_all(pieces, DP + TENSOR, 0, 0, axis_index_groups=groups)]
where the time goes in v5:
time: 95.4 us; the launch traced here: 95.1 us
  blocking collectives  87.9 us (92%)
  Pallas kernels  6.51 us (7%)
    all_to_all x1, blocking collectives, body(): pieces = lax.all_to_all(product(activations, out_grad, first), FIRST, 0, 0)  33.1 us
    all_to_all x1, blocking collectives, body(): message = lax.all_to_all(message, FIRST + TENSOR, 0, 0)  24.9 us
    all_to_all x1, blocking collectives, body(): pieces = lax.all_to_all(pieces, DP + TENSOR, 0, 0, axis_index_groups=groups)  20.7 us
    all_to_all x1, blocking collectives, body(): copies = lax.all_to_all(copies, FIRST, 0, 0)  9.19 us
    pallas_call x1, Pallas kernels, product(): pl.pallas_call(functools.partial(product_kernel, chunk, width), in_specs=...  5.17 us

profile of v5, /device:TPU:1, one launch (start us, length us, event | category | flops | bytes accessed | tf_op | source)
XLA Modules:
  0.0 95.1 jit_solution(3010786415868411350)
XLA Ops:
  0.6 5.2 %product.1 = f32[16,32,1024]{2,1,0:T(8,128)} custom-call(bf16[2000,512]{1,0:T(8,128)(2,1)} %act_hbm.1, bf16[2000,1024]{1,0:T(8,128)(2,1)} %cot_hbm.1), custom_call_target="tpu_custom_call" | custom-call | tf_op jit(solution)/shard_map/product/pallas_call | solution.py:76
  5.8 0.0 copy-start.2
  5.8 33.1 %all_to_all.20.pieces_ref = f32[16,32,1024]{2,1,0:T(8,128)S(1)} all-to-all(f32[16,32,1024]{2,1,0:T(8,128)} %product.1), channel_id=1, replica_groups=mesh['y_hi'=4,'y_lo'=2,'x'=4,'z_lo'=2,'z_hi'=4,'core'=2] {'z_lo','y_lo',..., dimensions={0} | all-to-all | bytes 4194304 | tf_op jit(solution)/shard_map/all_to_all | solution.py:188
  38.9 0.0 copy-done.2
  38.9 0.0 copy-start.1
  38.9 0.0 copy-start
  38.9 0.1 split.1
  39.0 20.7 %all_to_all.21.pieces_ref = f32[4,264,128]{2,1,0:T(8,128)S(1)} all-to-all(f32[4,264,128]{2,1,0:T(8,128)S(1)} %split.1), channel_id=1, replica_groups={{0,128,256,384},{385,257,129,1},{2,130,258,386},{387,259,131,3},{4,132,..., dimensions={0} | all-to-all | bytes 1081344 | tf_op jit(solution)/shard_map/all_to_all | solution.py:194
  59.8 0.1 columns.1
  59.8 9.2 %all_to_all.22.cols_ref = f32[16,1,1024]{2,1,0:T(1,128)S(1)} all-to-all(f32[16,1,1024]{2,1,0:T(1,128)S(1)} %get-tuple-element.15), channel_id=1, replica_groups=mesh['y_hi'=4,'y_lo'=2,'x'=4,'z_lo'=2,'z_hi'=4,'core'=2] {'z_lo','y_lo',..., dimensions={0} | all-to-all | bytes 131072 | tf_op jit(solution)/shard_map/all_to_all | solution.py:198
  69.0 0.0 copy-done.1
  69.0 0.2 rows.1
  69.2 24.9 %all_to_all.23.message_ref = f32[128,1,128]{2,1,0:T(1,128)S(1)} all-to-all(f32[128,1,128]{2,1,0:T(1,128)S(1)} %get-tuple-element.18), channel_id=1, replica_groups=mesh['y_hi'=4,'y_lo'=2,'x'=4,'z_lo'=2,'z_hi'=4,'core'=2] {'z_lo','y_lo',..., dimensions={0} | all-to-all | bytes 131072 | tf_op jit(solution)/shard_map/all_to_all | solution.py:205
  94.1 0.0 copy-done
  94.1 0.9 finish.1
Async XLA Ops:
  5.8 33.1 %copy-start.2 = (f32[8]{0:T(128)S(1)}, f32[8]{0:T(128)}, u32[]{:S(2)}) copy-start(f32[8]{0:T(128)} %param.8) | copy-start | bytes 100
  38.9 30.1 %copy-start.1 = (f32[1024]{0:T(1024)S(1)}, f32[1024]{0:T(1024)}, u32[]{:S(2)}) copy-start(f32[1024]{0:T(1024)} %param.9) | copy-start | bytes 12292
  38.9 55.2 %copy-start = (f32[8,1024]{1,0:T(8,128)S(1)}, f32[8,1024]{1,0:T(8,128)}, u32[]{:S(2)}) copy-start(f32[8,1024]{1,0:T(8,128)} %weight_ref.1) | copy-start | bytes 98308

commit v6 on v5

--- a/solution.py
+++ b/solution.py
@@ -195,7 +195,14 @@
     grad, moment, copies = call(
         column_kernel, [(rows, cols), (1, LANES), (first, 1, cols)], [VMEM], "columns"
     )(pieces)
-    copies = lax.all_to_all(copies, FIRST, 0, 0)
+    places = np.arange(math.prod(SIZES)).reshape(second, first, -1, SIZES[-1])
+    groups = [
+        [int(d) for d in places[i, :: 1 - 2 * core, j, core]]
+        for i in range(second)
+        for j in range(places.shape[2])
+        for core in range(SIZES[-1])
+    ]
+    copies = lax.all_to_all(copies, DP + TENSOR, 0, 0, axis_index_groups=groups)
     kept, message = call(
         functools.partial(row_kernel, all_rows, all_cols, tensor),
         [(1, cols), (first * tensor, 1, LANES)],

time: 95.4 us -> 95.4 us (level)
  no operation moved by 1% of the time
where the time goes in v6:
time: 95.4 us; the launch traced here: 95.1 us
  blocking collectives  87.9 us (92%)
  Pallas kernels  6.51 us (7%)
    all_to_all x1, blocking collectives, body(): pieces = lax.all_to_all(product(activations, out_grad, first), FIRST, 0, 0)  33.1 us
    all_to_all x1, blocking collectives, body(): message = lax.all_to_all(message, FIRST + TENSOR, 0, 0)  25.2 us
    all_to_all x1, blocking collectives, body(): pieces = lax.all_to_all(pieces, DP + TENSOR, 0, 0, axis_index_groups=groups)  20.7 us
    all_to_all x1, blocking collectives, body(): copies = lax.all_to_all(copies, DP + TENSOR, 0, 0, axis_index_groups=groups)  8.9 us
    pallas_call x1, Pallas kernels, product(): pl.pallas_call(functools.partial(product_kernel, chunk, width), in_specs=...  5.17 us

profile of v6, /device:TPU:1, one launch (start us, length us, event | category | flops | bytes accessed | tf_op | source)
XLA Modules:
  0.0 95.1 jit_solution(3931049759715060560)
XLA Ops:
  0.6 5.2 %product.1 = f32[16,32,1024]{2,1,0:T(8,128)} custom-call(bf16[2000,512]{1,0:T(8,128)(2,1)} %act_hbm.1, bf16[2000,1024]{1,0:T(8,128)(2,1)} %cot_hbm.1), custom_call_target="tpu_custom_call" | custom-call | tf_op jit(solution)/shard_map/product/pallas_call | solution.py:76
  5.8 0.0 copy-start.2
  5.8 33.1 %all_to_all.20.pieces_ref = f32[16,32,1024]{2,1,0:T(8,128)S(1)} all-to-all(f32[16,32,1024]{2,1,0:T(8,128)} %product.1), channel_id=1, replica_groups=mesh['y_hi'=4,'y_lo'=2,'x'=4,'z_lo'=2,'z_hi'=4,'core'=2] {'z_lo','y_lo',..., dimensions={0} | all-to-all | bytes 4194304 | tf_op jit(solution)/shard_map/all_to_all | solution.py:188
  38.9 0.0 copy-done.2
  38.9 0.0 copy-start.1
  38.9 0.0 copy-start
  38.9 0.1 split.1
  39.0 20.7 %all_to_all.21.pieces_ref = f32[4,264,128]{2,1,0:T(8,128)S(1)} all-to-all(f32[4,264,128]{2,1,0:T(8,128)S(1)} %split.1), channel_id=1, replica_groups={{0,128,256,384},{385,257,129,1},{2,130,258,386},{387,259,131,3},{4,132,..., dimensions={0} | all-to-all | bytes 1081344 | tf_op jit(solution)/shard_map/all_to_all | solution.py:194
  59.8 0.1 columns.1
  59.8 8.9 %all_to_all.22.cols_ref = f32[16,1,1024]{2,1,0:T(1,128)S(1)} all-to-all(f32[16,1,1024]{2,1,0:T(1,128)S(1)} %get-tuple-element.15), channel_id=1, replica_groups={{0,8,16,24,32,40,48,56,64,72,80,88,96,104,112,120},{121,113,105,97,89,8..., dimensions={0} | all-to-all | bytes 131072 | tf_op jit(solution)/shard_map/all_to_all | solution.py:205
  68.7 0.0 copy-done.1
  68.7 0.2 rows.1
  68.9 25.2 %all_to_all.23.message_ref = f32[128,1,128]{2,1,0:T(1,128)S(1)} all-to-all(f32[128,1,128]{2,1,0:T(1,128)S(1)} %get-tuple-element.18), channel_id=1, replica_groups=mesh['y_hi'=4,'y_lo'=2,'x'=4,'z_lo'=2,'z_hi'=4,'core'=2] {'z_lo','y_lo',..., dimensions={0} | all-to-all | bytes 131072 | tf_op jit(solution)/shard_map/all_to_all | solution.py:212
  94.1 0.0 copy-done
  94.1 0.9 finish.1
Async XLA Ops:
  5.8 33.1 %copy-start.2 = (f32[8]{0:T(128)S(1)}, f32[8]{0:T(128)}, u32[]{:S(2)}) copy-start(f32[8]{0:T(128)} %param.8) | copy-start | bytes 100
  38.9 29.8 %copy-start.1 = (f32[1024]{0:T(1024)S(1)}, f32[1024]{0:T(1024)}, u32[]{:S(2)}) copy-start(f32[1024]{0:T(1024)} %param.9) | copy-start | bytes 12292
  38.9 55.2 %copy-start = (f32[8,1024]{1,0:T(8,128)S(1)}, f32[8,1024]{1,0:T(8,128)}, u32[]{:S(2)}) copy-start(f32[8,1024]{1,0:T(8,128)} %weight_ref.1) | copy-start | bytes 98308
